TPU v7x, 32 devices: a whole 2x2x4 slice. The times are simulated.
32 devices in a mesh: grp: 2 (over y), inter: 4 (over z), intra: 4 (over x, core).
Axes of the slice: x: 2, y: 2, z: 4, core: 2. Of those that a mesh axis runs over, the one named last changes fastest.
Arguments:
- hidden: bfloat16 [4, 768, 8192], P('grp', 'inter', 'intra'), parts along dimension 0, may hold values from -20 to 20
- w_query: bfloat16 [8192, 4096], P('inter', 'intra'), may hold values from -2 to 2
- w_keyval: bfloat16 [8192, 1024], P('inter', 'intra'), may hold values from -1 to 1
- b_query: bfloat16 [4096], P('intra'), may hold values from -3 to 3
- b_keyval: bfloat16 [1024], P('intra'), may hold values from -3 to 3
- segments: int32 [4, 4, 192], P('grp', 'inter'), parts along dimension 0, may hold values from 0 to 8, never falling along the last dimension, each value on 1 to 48 neighbouring positions
Outputs:
- context: bfloat16 [4, 768, 4096], P('grp', 'inter', 'intra'), parts along dimension 0
There are 2 independent parts, one for each index of `grp`. A program takes and returns all parts, laid end to end along the dimension named above; an argument that names none is the same for every part. Nothing has to cross between parts.
Inputs may be any that keep to these rules, and one draw needn't show every extreme that they name: `segments`: in every block the segment numbers never fall, every number of 0 to 8 occurs, and each segment has 1 to 48 tokens.
All inputs are finite; a program needn't handle non-finite values.
Results may differ from a plain program's by a relative error of at most 0.0075.
Values may be sent and summed in bfloat16 or wider, within the bound.
A program may use at most 128 MiB of HBM per device.

v0:
```python
import jax
import jax.numpy as jnp
from jax import lax
from jax.sharding import PartitionSpec as P

QH = 32
KV = 4
HD = 128


def positions(segments):
    prefix = jnp.sum((segments == 0).astype(jnp.int32), axis=-1, keepdims=True)
    below = jnp.sum((segments[..., None, :] < segments[..., :, None]).astype(jnp.int32), axis=-1)
    places = lax.broadcasted_iota(jnp.int32, segments.shape, segments.ndim - 1)
    return places - below + jnp.where(segments > 0, prefix, 0)


def rotate(values, angles_pos):
    width = values.shape[-1]
    half = width // 2
    freq = 1000000.0 ** (-2.0 * jnp.arange(half, dtype=jnp.float32) / width)
    angles = angles_pos[..., None] * freq
    cosine = jnp.cos(angles)
    sine = jnp.sin(angles)
    first = values[..., :half]
    second = values[..., half:]
    return jnp.concatenate(
        [first * cosine - second * sine, second * cosine + first * sine], axis=-1
    )


def add_rows(flat, piece):
    return jnp.dot(flat, piece, preferred_element_type=jnp.float32)


def local(hidden, w_query, w_keyval, b_query, b_keyval, segments):
    batches, block_len, _ = hidden.shape
    whole = jnp.stack(
        [lax.all_gather(hidden[batch], "intra", axis=1, tiled=True) for batch in range(batches)],
        axis=0,
    )
    rows = batches * block_len
    flat = whole.reshape(rows, whole.shape[2])

    def add_one(piece):
        return add_rows(flat, piece)

    query = add_one(lax.all_gather(w_query, "inter", axis=0, tiled=True))
    keyval = add_one(lax.all_gather(w_keyval, "inter", axis=0, tiled=True))
    query = query + b_query.astype(jnp.float32)
    keyval = keyval + b_keyval.astype(jnp.float32)
    seg_local = segments.reshape(batches, block_len)
    place_pos = positions(seg_local).reshape(rows).astype(jnp.float32)
    head_dim = HD
    local_heads = query.shape[1] // head_dim
    query = rotate(query.reshape(rows, local_heads, head_dim), place_pos[:, None]).astype(
        jnp.bfloat16
    )
    blocks_here = keyval.shape[1] // head_dim
    kv_split = keyval.reshape(rows, blocks_here, head_dim)
    rotated = rotate(kv_split, place_pos[:, None])
    device = lax.axis_index("intra")
    global_block = device * blocks_here + jnp.arange(blocks_here, dtype=jnp.int32)
    kv_ready = jnp.where((global_block < KV)[None, :, None], rotated, kv_split).astype(jnp.bfloat16)
    kv_ready = kv_ready.reshape(rows, blocks_here * head_dim)
    kv_all = lax.all_gather(kv_ready, "intra", axis=1, tiled=True)
    group = QH // KV
    kv_head = device * local_heads // group
    keys = lax.dynamic_slice_in_dim(kv_all, kv_head * head_dim, head_dim, 1)
    values = lax.dynamic_slice_in_dim(kv_all, (KV + kv_head) * head_dim, head_dim, 1)
    query = query.reshape(batches, block_len, local_heads, head_dim)
    keys = keys.reshape(batches, block_len, head_dim)
    values = values.reshape(batches, block_len, head_dim)
    scores = jnp.einsum(
        "btgd,bsd->bgts", query, keys, preferred_element_type=jnp.float32
    ) * head_dim ** (-0.5)
    later = jnp.arange(block_len, dtype=jnp.int32)
    causal = later[None, :] <= later[:, None]
    same = (seg_local[:, None, :] == 0) | (seg_local[:, None, :] == seg_local[:, :, None])
    allowed = (causal[None] & same)[:, None, :, :]
    scores = jnp.where(allowed, scores, -1e30)
    peak = jnp.max(scores, axis=-1, keepdims=True)
    expo = jnp.where(allowed, jnp.exp(scores - peak), 0.0)
    weights = (expo / jnp.sum(expo, axis=-1, keepdims=True)).astype(jnp.bfloat16)
    context = jnp.einsum("bgts,bsd->btgd", weights, values, preferred_element_type=jnp.float32)
    return context.reshape(batches, block_len, local_heads * head_dim).astype(jnp.bfloat16)


def solution(mesh):
    in_specs = (
        P("grp", "inter", "intra"),
        P("inter", "intra"),
        P("inter", "intra"),
        P("intra"),
        P("intra"),
        P("grp", "inter", None),
    )
    out_specs = P("grp", "inter", "intra")
    return jax.shard_map(local, mesh=mesh, in_specs=in_specs, out_specs=out_specs, check_vma=False)
```

profile of v0, /device:TPU:9, one launch (start us, length us, event | category | flops | bytes accessed | tf_op | source)
XLA Modules:
  0.0 460.4 jit_solution(3109908411917099399)
XLA Ops:
  6.5 2.7 fusion.17
  9.3 0.7 all-gather.11.cloned.1.call-update
  10.1 0.7 all-gather.7.cloned.1.call-update
  10.8 0.5 all-gather.9.cloned.1.call-update
  12.4 0.4 multiply_cosine_fusion
  12.8 26.7 %all-gather.13.cloned.1.call-done = bf16[1,192,8192]{2,1,0:T(8,128)(2,1)} async-done(((bf16[1,192,2048]{2,1,0:T(8,128)(2,1)}), bf16[1,192,8192]{2,1,0:T(8,128)(2,1)}) %all-gather.13.cloned.1.call-update) | async-done | bytes 3145744 | tf_op jit(solution)/shard_map/all_gather | solution.py:39
  39.5 30.1 %all-gather.11.cloned.1.call-done = bf16[1,192,8192]{2,1,0:T(8,128)(2,1)} async-done(((bf16[1,192,2048]{2,1,0:T(8,128)(2,1)}), bf16[1,192,8192]{2,1,0:T(8,128)(2,1)}) %all-gather.11.cloned.1.call-update) | async-done | bytes 3145744 | tf_op jit(solution)/shard_map/all_gather | solution.py:39
  69.6 6.1 %pad_maximum_fusion = bf16[2,192,8192]{2,1,0:T(8,128)(2,1)} fusion(bf16[1,192,8192]{2,1,0:T(8,128)(2,1)} %all-gather.13.cloned.1.call-done, bf16[1,192,8192]{2,1,0:T(8,128)(2,1)} %all-gather.11.cloned.1.call-done), kind=kLoop, calls=%fused_computation.1 | loop fusion | flops 3145728 | bytes 12582912 | tf_op jit(solution)/shard_map/stack | solution.py:38
  75.7 73.4 %all-gather.7.cloned.1.call-done = bf16[8192,256]{1,0:T(8,128)(2,1)} async-done(((bf16[2048,256]{1,0:T(8,128)(2,1)}), bf16[8192,256]{1,0:T(8,128)(2,1)}) %all-gather.7.cloned.1.call-update) | async-done | bytes 4194320 | tf_op jit(solution)/shard_map/all_gather | solution.py:49
  149.1 6.5 %convolution_add_fusion.1 = f32[384,256]{0,1:T(8,128)S(1)} fusion(bf16[384,8192]{1,0:T(8,128)(2,1)} %bitcast.54, bf16[8192,256]{1,0:T(8,128)(2,1)} %all-gather.7.cloned.1.call-done, f32[256]{0:T(256)S(1)} %convert_element_type.37), kind=kOutput, calls=%fused_computation.13 | convolution fusion | flops 1610711040 | bytes 10880000 | tf_op jit(solution)/shard_map/dot_general | solution.py:33
  155.8 9.2 %all_gather.18 = bf16[384,1024]{0,1:T(8,128)(2,1)S(1)} all-gather(bf16[384,256]{0,1:T(8,128)(2,1)S(1)} %fusion.12), channel_id=1, replica_groups=mesh['grp'=2,'inter'=4,'intra'=4] {'intra'}, dimensions={1}, use_global_device_ids=true | all-gather | bytes 983040 | tf_op jit(solution)/shard_map/all_gather | solution.py:66
  165.0 0.8 copy.10
  165.8 269.7 %all-gather.9.cloned.1.call-done = bf16[8192,1024]{1,0:T(8,128)(2,1)} async-done(((bf16[2048,1024]{1,0:T(8,128)(2,1)}), bf16[8192,1024]{1,0:T(8,128)(2,1)}) %all-gather.9.cloned.1.call-update) | async-done | bytes 16777232 | tf_op jit(solution)/shard_map/all_gather | solution.py:48
  435.5 12.0 %convolution_add_fusion = f32[384,1024]{1,0:T(8,128)S(1)} fusion(bf16[384,8192]{1,0:T(8,128)(2,1)} %bitcast.55, bf16[8192,1024]{1,0:T(8,128)(2,1)} %all-gather.9.cloned.1.call-done, f32[1024]{0:T(1024)S(1)} %convert_element_type.42), kind=kOutput, calls=%fused_computation.10 | convolution fusion | flops 6442844160 | bytes 24645632 | tf_op jit(solution)/shard_map/dot_general | solution.py:33
  447.6 0.5 copy.21
  448.1 0.2 subtract_convert_fusion
  448.3 0.3 concatenate.17
  448.6 0.6 copy.15
  449.2 0.3 concatenate.16
  449.4 0.6 copy.14
  450.0 0.7 fusion.8
  450.7 1.2 fusion.18
  451.9 0.8 fusion.7
  452.8 1.1 copy.30
  (36 shorter events, 1.4 us)
Async XLA Ops:
  6.5 33.0 %all-gather.13.cloned.1.call-start = ((), (), s32[]{:S(2)}) async-start(), calls=%async_computation.3 | async-start | bytes 3932160 | tf_op jit(solution)/shard_map/all_gather | solution.py:39
  9.3 2.1 copy-start.3
  9.3 2.1 copy-start.1
  9.3 2.8 copy-start.2
  9.3 60.3 %all-gather.11.cloned.1.call-start = ((), (), s32[]{:S(2)}) async-start(), calls=%async_computation.2 | async-start | bytes 3932160 | tf_op jit(solution)/shard_map/all_gather | solution.py:39
  10.0 139.0 %all-gather.7.cloned.1.call-start = ((), (), s32[]{:S(2)}) async-start(), calls=%async_computation | async-start | bytes 5242880 | tf_op jit(solution)/shard_map/all_gather | solution.py:49
  10.8 424.8 %all-gather.9.cloned.1.call-start = ((), (), s32[]{:S(2)}) async-start(), calls=%async_computation.1 | async-start | bytes 20971520 | tf_op jit(solution)/shard_map/all_gather | solution.py:48
  450.7 1.2 copy-start
Sparse Core Ops, SparseCore 0:
  9.4 30.0 all-gather.12
  41.1 28.5 all-gather.10
  71.2 77.8 all-gather.6
  150.5 284.9 all-gather.8
where the time goes:
time: 465 us; the launch traced here: 460 us
  waiting for transfers between devices  402 us (86%)
  matrix products  20 us (4%)
  between operations  13.4 us (3%)
  blocking collectives  9.17 us (2%)
  other arithmetic  8.62 us (2%)
  local copies, waits for them, and re-layouts  7.28 us (2%)
    all_gather x1, waiting for transfers between devices, local(): query = add_one(lax.all_gather(w_query, 'inter', axis=0, tiled=True))  270 us
    all_gather x1, waiting for transfers between devices, local(): keyval = add_one(lax.all_gather(w_keyval, 'inter', axis=0, tiled=True))  73.4 us
    all_gather x2, waiting for transfers between devices, local(): lax.all_gather(hidden[batch], 'intra', axis=1, tiled=True)  56.8 us
    dot_general x2, matrix products, add_rows(): return jnp.dot(flat, piece, preferred_element_type=jnp.float32)  18.5 us
  transfers between devices with their start and end apart: 4, of which 4 were waited for; matrix products, arithmetic and copies ran while one was open for 3% of the time, Pallas kernels for 0%

commit v1 on v0

v1 whole, which is shorter than its diff:
```python
import functools

import jax
import jax.numpy as jnp
import numpy as np
from jax import lax
from jax.experimental import pallas as pl
from jax.experimental.pallas import tpu as pltpu
from jax.sharding import PartitionSpec as P

QH = 32
KV = 4
HD = 128
CORES = 2
MESH = pl.DeviceIdType.MESH


def kernel(n_inter, n_intra, hid, wq, wkv, bq, bkv, seg, freq, out,
           xg, wbuf, rb, cosb, sinb, maskb, kvs, kvb,
           wsem, hsend, hrecv, fsend, xsend, frecv, csend, crecv, kvsend, kvrecv):
    batches, block = seg.shape
    rows = batches * block
    depth = wkv.shape[0]
    width = wkv.shape[1]
    chunks = wbuf.shape[0]
    piece = rows // n_intra
    layers_each = n_inter // n_intra
    chips = n_intra // CORES
    i = lax.axis_index("inter")
    j = lax.axis_index("intra")
    xc = j // CORES
    core = lax.rem(j, CORES)
    sibling = xc * CORES + (CORES - 1 - core)
    total = n_inter * n_intra
    me = i * n_intra + j

    wcopies = [pltpu.make_async_copy(wkv, wbuf.at[0], wsem.at[0])]
    for c in range(chunks - 1):
        wcopies.append(pltpu.make_async_copy(
            wq.at[:, pl.ds(c * width, width)], wbuf.at[c + 1], wsem.at[c + 1]))
    for cp in wcopies:
        cp.start()

    barrier = pltpu.get_barrier_semaphore()

    @pl.loop(1, total)
    def _(k):
        other = lax.rem(me + k, total)
        pl.semaphore_signal(
            barrier, inc=1,
            device_id={"inter": other // n_intra, "intra": lax.rem(other, n_intra)},
            device_id_type=MESH)

    pl.semaphore_wait(barrier, total - 1)

    def remote(src, dst, ssem, rsem, ii, jj):
        return pltpu.make_async_remote_copy(
            src_ref=src, dst_ref=dst, send_sem=ssem, recv_sem=rsem,
            device_id={"inter": ii, "intra": jj}, device_id_type=MESH)

    def spread(gg, p):
        src = hid.at[pl.ds(p * piece, piece), pl.ds(gg * depth, depth)]
        dst = xg.at[i, pl.ds(p * piece, piece), :]
        return src, dst

    for gg in range(layers_each):
        layer = j * layers_each + gg
        for p in range(n_intra):
            src, dst = spread(gg, p)
            here = (layer == i) & (p == j)

            @pl.when(here)
            def _():
                pltpu.make_async_copy(src, dst, hrecv.at[i]).start()

            @pl.when(jnp.logical_not(here))
            def _():
                remote(src, dst, hsend.at[gg * n_intra + p], hrecv.at[i], layer, p).start()

    def part(t, p):
        return xg.at[t, pl.ds(pl.multiple_of(p * piece, piece), piece), :]

    fr = freq[...]
    lane = lax.broadcasted_iota(jnp.int32, (1, HD), 1)
    r_i = lax.broadcasted_iota(jnp.int32, (block, block), 0)
    c_i = lax.broadcasted_iota(jnp.int32, (block, block), 1)
    place = lax.broadcasted_iota(jnp.int32, (block, 1), 0).astype(jnp.float32)

    def tables():
        for b in range(batches):
            segr = seg[b:b + 1, :].astype(jnp.float32)
            segm = jnp.broadcast_to(segr, (block, block))
            segc = jnp.sum(jnp.where(r_i == c_i, segm, 0.0), axis=1, keepdims=True)
            below = jnp.sum(jnp.where(segm < segc, 1.0, 0.0), axis=1, keepdims=True)
            plen = jnp.sum(jnp.where(segm == 0.0, 1.0, 0.0), axis=1, keepdims=True)
            pos = place - below + jnp.where(segc > 0.0, plen, 0.0)
            angles = pos * fr
            cosb[b * block:(b + 1) * block, :] = jnp.cos(angles)
            sine = jnp.sin(angles)
            sinb[b * block:(b + 1) * block, :] = jnp.where(lane < HD // 2, -sine, sine)
            allowed = (c_i <= r_i) & ((segm == 0.0) | (segm == segc))
            maskb[b] = jnp.where(allowed, 0.0, -1e30)

    def own_copies(t):
        res = []
        for k in range(1, chips):
            ox = lax.rem(xc + k, chips)
            res.append(remote(part(t, j), part(t, j), fsend.at[t, k], frecv.at[t, j],
                              i, ox * CORES + core))
        res.append(remote(part(t, j), part(t, j), fsend.at[t, 0], frecv.at[t, j], i, sibling))
        return res

    def cross_copies(t):
        res = []
        for k in range(1, chips):
            p = lax.rem(xc + k, chips) * CORES + core
            res.append(remote(part(t, p), part(t, p), xsend.at[t, k - 1], frecv.at[t, p],
                              i, sibling))
        return res

    def arrived(t, p):
        pltpu.make_async_copy(part(t, p), part(t, p), frecv.at[t, p]).wait()

    def order(k):
        return lax.rem(i + k, n_inter)

    @pl.loop(0, n_inter + 1)
    def _(k):
        @pl.when(k < n_inter)
        def _():
            t = order(k)
            pltpu.make_async_copy(part(t, j), part(t, j), hrecv.at[t]).wait()
            for cp in own_copies(t):
                cp.start()

        @pl.when(k == 0)
        def _():
            tables()

        @pl.when(k > 0)
        def _():
            t = order(k - 1 + n_inter)
            for q in range(1, chips):
                arrived(t, lax.rem(xc + q, chips) * CORES + core)
            for cp in cross_copies(t):
                cp.start()

    for cp in wcopies:
        cp.wait()

    def ready(t):
        for q in range(chips):
            arrived(t, q * CORES + (CORES - 1 - core))

    def product(t, c):
        return jnp.dot(xg[t], wbuf[c], preferred_element_type=jnp.float32)

    def chain(t, c, slot, to):
        return remote(rb.at[t, c], rb.at[slot, c], csend.at[t, c], crecv.at[slot, c], to, j)

    def landed(slot, c):
        pltpu.make_async_copy(rb.at[slot, c], rb.at[slot, c], crecv.at[slot, c]).wait()

    def hop(t, c, has_before, slot, to):
        acc = product(t, c)

        @pl.when(has_before)
        def _():
            landed(t, c)
            rb[t, c] = (rb[t, c].astype(jnp.float32) + acc).astype(jnp.bfloat16)

        @pl.when(jnp.logical_not(has_before))
        def _():
            rb[t, c] = acc.astype(jnp.bfloat16)

        chain(t, c, slot, to).start()

    def down_slot(t):
        return jnp.where(t == i - 1, n_inter, t)

    @pl.loop(0, n_inter - 1)
    def _(s):
        up = n_inter - 1 - s
        down = s

        @pl.when(up > i)
        def _():
            ready(up)

        @pl.when(down < i)
        def _():
            ready(down)

        @pl.loop(0, chunks)
        def _(c):
            @pl.when(up > i)
            def _():
                hop(up, c, i > 0, up, i + 1)

            @pl.when(down < i)
            def _():
                hop(down, c, i < n_inter - 1, down_slot(down), i - 1)

    ready(i)

    def total_of(c):
        acc = product(i, c)
        zero = jnp.zeros_like(acc)

        @pl.when(i > 0)
        def _():
            landed(i, c)

        @pl.when(i < n_inter - 1)
        def _():
            landed(n_inter, c)

        acc = acc + jnp.where(i > 0, rb[i, c].astype(jnp.float32), zero)
        return acc + jnp.where(i < n_inter - 1, rb[n_inter, c].astype(jnp.float32), zero)

    def rot(u):
        return u * cosb[...] + pltpu.roll(u, HD // 2, 1) * sinb[...]

    @pl.when(i == 0)
    def _():
        rb[0] = jnp.zeros(rb.shape[1:], rb.dtype)

    @pl.when(i == n_inter - 1)
    def _():
        rb[n_inter] = jnp.zeros(rb.shape[1:], rb.dtype)

    here_kv = width // HD
    per = n_intra // KV
    acc = total_of(0) + bkv[...].astype(jnp.float32)
    for b in range(here_kv):
        gb = j * here_kv + b
        u = acc[:, b * HD:(b + 1) * HD]
        kvs[b] = jnp.where(gb < KV, rot(u), u).astype(jnp.bfloat16)

    def kv_copies(b, r):
        gb = j * here_kv + b
        dest = lax.rem(gb, KV) * per + r
        kind = gb // KV
        return dest, kind, remote(kvs.at[b], kvb.at[kind], kvsend.at[b * per + r],
                                  kvrecv.at[kind], i, dest)

    for b in range(here_kv):
        for r in range(per):
            dest, kind, cp = kv_copies(b, r)

            @pl.when(dest == j)
            def _():
                pltpu.make_async_copy(kvs.at[b], kvb.at[kind], kvrecv.at[kind]).start()

            @pl.when(dest != j)
            def _():
                cp.start()

    for kind in range(2):
        pltpu.make_async_copy(kvb.at[kind], kvb.at[kind], kvrecv.at[kind]).wait()

    for c in range(1, chunks):
        base = (c - 1) * width
        acc = total_of(c) + bq[:, base:base + width].astype(jnp.float32)
        for h in range(width // HD):
            qh = rot(acc[:, h * HD:(h + 1) * HD]).astype(jnp.bfloat16)
            for b in range(batches):
                lo = b * block
                sc = lax.dot_general(qh[lo:lo + block, :], kvb[0, lo:lo + block, :],
                                     (((1,), (1,)), ((), ())),
                                     preferred_element_type=jnp.float32)
                sc = sc * HD ** (-0.5) + maskb[b]
                peak = jnp.max(sc, axis=-1, keepdims=True)
                expo = jnp.exp(sc - peak)
                wts = (expo / jnp.sum(expo, axis=-1, keepdims=True)).astype(jnp.bfloat16)
                ctx = jnp.dot(wts, kvb[1, lo:lo + block, :], preferred_element_type=jnp.float32)
                out[lo:lo + block, base + h * HD:base + (h + 1) * HD] = ctx.astype(jnp.bfloat16)

    for gg in range(layers_each):
        layer = j * layers_each + gg
        for p in range(n_intra):
            src, dst = spread(gg, p)

            @pl.when(jnp.logical_not((layer == i) & (p == j)))
            def _():
                remote(src, dst, hsend.at[gg * n_intra + p], hrecv.at[i], layer, p).wait_send()

    @pl.loop(0, n_inter)
    def _(t):
        for cp in own_copies(t) + cross_copies(t):
            cp.wait_send()

        @pl.when(t != i)
        def _():
            @pl.loop(0, chunks)
            def _(c):
                chain(t, c, t, i).wait_send()

    for b in range(here_kv):
        for r in range(per):
            dest, kind, cp = kv_copies(b, r)

            @pl.when(dest != j)
            def _():
                cp.wait_send()


def local(n_inter, n_intra, hidden, w_query, w_keyval, b_query, b_keyval, segments):
    batches, block, feats = hidden.shape
    rows = batches * block
    depth, cols = w_query.shape
    width = w_keyval.shape[1]
    chunks = 1 + cols // width
    chips = n_intra // CORES
    half = HD // 2
    fr = 1000000.0 ** (-2.0 * np.arange(half, dtype=np.float64) / HD)
    freq = jnp.asarray(np.concatenate([fr, fr])[None, :], jnp.float32)
    vmem = pl.BlockSpec(memory_space=pltpu.VMEM)
    hbm = pl.BlockSpec(memory_space=pl.ANY)
    dma = pltpu.SemaphoreType.DMA
    here_kv = width // HD
    per = n_intra // KV
    result = pl.pallas_call(
        functools.partial(kernel, n_inter, n_intra),
        out_shape=jax.ShapeDtypeStruct((rows, cols), jnp.bfloat16),
        in_specs=[hbm, hbm, hbm, vmem, vmem, vmem, vmem],
        out_specs=vmem,
        scratch_shapes=[
            pltpu.VMEM((n_inter, rows, depth), jnp.bfloat16),
            pltpu.VMEM((chunks, depth, width), jnp.bfloat16),
            pltpu.VMEM((n_inter + 1, chunks, rows, width), jnp.bfloat16),
            pltpu.VMEM((rows, HD), jnp.float32),
            pltpu.VMEM((rows, HD), jnp.float32),
            pltpu.VMEM((batches, block, block), jnp.float32),
            pltpu.VMEM((here_kv, rows, HD), jnp.bfloat16),
            pltpu.VMEM((2, rows, HD), jnp.bfloat16),
            dma((chunks,)),
            dma((n_intra * (n_inter // n_intra),)),
            dma((n_inter,)),
            dma((n_inter, chips)),
            dma((n_inter, max(chips - 1, 1))),
            dma((n_inter, n_intra)),
            dma((n_inter, chunks)),
            dma((n_inter + 1, chunks)),
            dma((here_kv * per,)),
            dma((2,)),
        ],
        compiler_params=pltpu.CompilerParams(
            collective_id=0, has_side_effects=True, vmem_limit_bytes=52 * 2**20),
        name="project_attend",
    )(hidden.reshape(rows, feats), w_query, w_keyval, b_query[None, :], b_keyval[None, :],
      segments.reshape(batches, block), freq)
    return result.reshape(batches, block, cols)


def solution(mesh):
    in_specs = (
        P("grp", "inter", "intra"),
        P("inter", "intra"),
        P("inter", "intra"),
        P("intra"),
        P("intra"),
        P("grp", "inter", None),
    )
    out_specs = P("grp", "inter", "intra")
    body = functools.partial(local, mesh.shape["inter"], mesh.shape["intra"])
    return jax.shard_map(body, mesh=mesh, in_specs=in_specs, out_specs=out_specs, check_vma=False)
```

time: 465 us -> 173 us (0.37)
  waiting for transfers between devices: 402 us -> 0 us
  Pallas kernels: 0 us -> 167 us
  matrix products: 20 us -> 0 us
  between operations: 13.4 us -> 0.01 us
  blocking collectives: 9.17 us -> 0 us
  other arithmetic: 8.62 us -> 0 us
    all_gather x4 -> x0, waiting for transfers between devices: 400 us -> none  [the longest x1 270 us: local(): query = add_one(lax.all_gather(w_query, 'inter', axis=0, tiled=True))]
    pallas_call x0 -> x1, Pallas kernels: none -> 167 us  [local(): pl.pallas_call(functools.partial(kernel, n_inter, n_intra), out_shape=jax...]
    dot_general x4 -> x0, matrix products: 20 us -> none  [the longest x2 18.5 us: add_rows(): return jnp.dot(flat, piece, preferred_element_type=jnp.float32)]
    all_gather x1 -> x0, blocking collectives: 9.17 us -> none  [local(): kv_all = lax.all_gather(kv_ready, 'intra', axis=1, tiled=True)]
    another operation x2 -> x0, other arithmetic: 6.3 us -> none  [the longest x1 6.08 us: local(): jnp.stack([lax.all_gather(hidden[batch], 'intra', axis=1, tiled=True) for...]
  transfers between devices with their start and end apart: 4 -> 0, of which waited for: 4 -> 0; matrix products, arithmetic and copies ran while one was open for 3% -> 0% of each run, Pallas kernels for 0% -> 0%
where the time goes in v1:
time: 173 us; the launch traced here: 172 us
  Pallas kernels  167 us (97%)
  local copies, waits for them, and re-layouts  4.79 us (3%)
    pallas_call x1, Pallas kernels, local(): pl.pallas_call(functools.partial(kernel, n_inter, n_intra), out_shape=jax...  167 us

profile of v1, /device:TPU:9, one launch (start us, length us, event | category | flops | bytes accessed | tf_op | source)
XLA Modules:
  0.0 171.8 jit_solution(12405011138271467559)
XLA Ops:
  0.0 0.7 broadcast_in_dim.7.bkv
  0.7 0.7 copy.10
  1.3 0.7 broadcast_in_dim.6.bq
  2.0 0.0 copy-start
  2.0 1.2 copy-done
  3.3 0.0 copy-start.1
  3.3 0.7 copy-done.1
  3.9 167.0 %project_attend.1 = bf16[384,1024]{1,0:T(8,128)(2,1)S(1)} custom-call(bf16[384,2048]{1,0:T(8,128)(2,1)} %bitcast.7, bf16[2048,1024]{1,0:T(8,128)(2,1)} %wq.1, bf16[2048,256]{1,0:T(8,128)(2,1)S(1)} %copy-done, bf16[1,1024]{1,0:T(2,128)(2,1)S(1)} %broadcast_in_dim.6.bq, bf16[1,256]{1,0:T(2,128)(2,1)S(1)} %broadcast_in_dim.7.bkv, s32[2,192]{1,0:T(2,128)S(1)} %bitcast.6, ...), custom_call_target="tpu_custom_call" | custom-call | tf_op jit(solution)/shard_map/project_attend/pallas_call | solution.py:323
  170.9 0.9 copy.12
Async XLA Ops:
  2.0 1.2 copy-start
  3.3 0.7 copy-start.1

commit v2 on v1

--- a/solution.py
+++ b/solution.py
@@ -1,8 +1,8 @@
 import functools
+import math
 
 import jax
 import jax.numpy as jnp
-import numpy as np
 from jax import lax
 from jax.experimental import pallas as pl
 from jax.experimental.pallas import tpu as pltpu
@@ -12,13 +12,14 @@
 KV = 4
 HD = 128
 CORES = 2
+FALL = -2.0 * math.log(1000000.0) / HD
 MESH = pl.DeviceIdType.MESH
 
 
-def kernel(n_inter, n_intra, hid, wq, wkv, bq, bkv, seg, freq, out,
-           xg, wbuf, rb, cosb, sinb, maskb, kvs, kvb,
-           wsem, hsend, hrecv, fsend, xsend, frecv, csend, crecv, kvsend, kvrecv):
-    batches, block = seg.shape
+def kernel(n_inter, n_intra, hid, wq, wkv, bq, bkv, seg, out,
+           xg, stage, wbuf, rb, cosb, sinb, maskb, kvs, kvb,
+           wsem, hsend, srecv, zsend, hrecv, fsend, xsend, frecv, csend, crecv, kvsend, kvrecv):
+    batches, _, block = seg.shape
     rows = batches * block
     depth = wkv.shape[0]
     width = wkv.shape[1]
@@ -59,36 +60,72 @@
             device_id={"inter": ii, "intra": jj}, device_id_type=MESH)
 
     def spread(gg, p):
+        layer = j * layers_each + gg
         src = hid.at[pl.ds(p * piece, piece), pl.ds(gg * depth, depth)]
-        dst = xg.at[i, pl.ds(p * piece, piece), :]
-        return src, dst
+        final = xg.at[i, pl.ds(p * piece, piece), :]
+        sem = hsend.at[gg * n_intra + p]
+        direct = remote(src, final, sem, hrecv.at[i], layer, p)
+        detour = remote(src, stage.at[layer], sem, srecv.at[layer], i, p)
+        keep = pltpu.make_async_copy(src, final, hrecv.at[i])
+        here = (layer == i) & (p == j)
+        straight = jnp.logical_not(here) & ((layer == i) | (p // CORES == xc))
+        return here, straight, keep, direct, detour
 
     for gg in range(layers_each):
-        layer = j * layers_each + gg
         for p in range(n_intra):
-            src, dst = spread(gg, p)
-            here = (layer == i) & (p == j)
+            here, straight, keep, direct, detour = spread(gg, p)
 
             @pl.when(here)
             def _():
-                pltpu.make_async_copy(src, dst, hrecv.at[i]).start()
-
-            @pl.when(jnp.logical_not(here))
-            def _():
-                remote(src, dst, hsend.at[gg * n_intra + p], hrecv.at[i], layer, p).start()
+                keep.start()
+
+            @pl.when(straight)
+            def _():
+                direct.start()
+
+            @pl.when(jnp.logical_not(here | straight))
+            def _():
+                detour.start()
 
     def part(t, p):
         return xg.at[t, pl.ds(pl.multiple_of(p * piece, piece), piece), :]
 
-    fr = freq[...]
+    def along(t):
+        return remote(stage.at[t], part(i, j), zsend.at[t], hrecv.at[i], t, j)
+
+    def detoured(t):
+        return (t // layers_each) // CORES != xc
+
+    def each(s, fn):
+        up = n_inter - 1 - s
+
+        @pl.when((s >= 0) & (up > i))
+        def _():
+            fn(up)
+
+        @pl.when((s >= 0) & (s < i))
+        def _():
+            fn(s)
+
+    def onward(t):
+        @pl.when(detoured(t))
+        def _():
+            pltpu.make_async_copy(stage.at[t], stage.at[t], srecv.at[t]).wait()
+            along(t).start()
+
+    @pl.loop(0, n_inter - 1)
+    def _(s):
+        each(s, onward)
+
     lane = lax.broadcasted_iota(jnp.int32, (1, HD), 1)
+    fr = jnp.exp(lax.rem(lane, HD // 2).astype(jnp.float32) * FALL)
     r_i = lax.broadcasted_iota(jnp.int32, (block, block), 0)
     c_i = lax.broadcasted_iota(jnp.int32, (block, block), 1)
     place = lax.broadcasted_iota(jnp.int32, (block, 1), 0).astype(jnp.float32)
 
     def tables():
         for b in range(batches):
-            segr = seg[b:b + 1, :].astype(jnp.float32)
+            segr = seg[b].astype(jnp.float32)
             segm = jnp.broadcast_to(segr, (block, block))
             segc = jnp.sum(jnp.where(r_i == c_i, segm, 0.0), axis=1, keepdims=True)
             below = jnp.sum(jnp.where(segm < segc, 1.0, 0.0), axis=1, keepdims=True)
@@ -121,29 +158,18 @@
     def arrived(t, p):
         pltpu.make_async_copy(part(t, p), part(t, p), frecv.at[t, p]).wait()
 
-    def order(k):
-        return lax.rem(i + k, n_inter)
-
-    @pl.loop(0, n_inter + 1)
-    def _(k):
-        @pl.when(k < n_inter)
-        def _():
-            t = order(k)
-            pltpu.make_async_copy(part(t, j), part(t, j), hrecv.at[t]).wait()
-            for cp in own_copies(t):
-                cp.start()
-
-        @pl.when(k == 0)
-        def _():
-            tables()
-
-        @pl.when(k > 0)
-        def _():
-            t = order(k - 1 + n_inter)
-            for q in range(1, chips):
-                arrived(t, lax.rem(xc + q, chips) * CORES + core)
-            for cp in cross_copies(t):
-                cp.start()
+    def own(t):
+        pltpu.make_async_copy(part(t, j), part(t, j), hrecv.at[t]).wait()
+        for cp in own_copies(t):
+            cp.start()
+
+    def cross(t):
+        for q in range(1, chips):
+            arrived(t, lax.rem(xc + q, chips) * CORES + core)
+        for cp in cross_copies(t):
+            cp.start()
+
+    tables()
 
     for cp in wcopies:
         cp.wait()
@@ -178,18 +204,10 @@
     def down_slot(t):
         return jnp.where(t == i - 1, n_inter, t)
 
-    @pl.loop(0, n_inter - 1)
-    def _(s):
+    def sums(s):
         up = n_inter - 1 - s
-        down = s
-
-        @pl.when(up > i)
-        def _():
-            ready(up)
-
-        @pl.when(down < i)
-        def _():
-            ready(down)
+
+        each(s, ready)
 
         @pl.loop(0, chunks)
         def _(c):
@@ -197,9 +215,33 @@
             def _():
                 hop(up, c, i > 0, up, i + 1)
 
-            @pl.when(down < i)
-            def _():
-                hop(down, c, i < n_inter - 1, down_slot(down), i - 1)
+            @pl.when(s < i)
+            def _():
+                hop(s, c, i < n_inter - 1, down_slot(s), i - 1)
+
+    last = n_inter - 1
+
+    @pl.loop(0, n_inter + 1)
+    def _(s):
+        @pl.when(s < last)
+        def _():
+            each(s, own)
+
+        @pl.when(s == last)
+        def _():
+            own(i)
+
+        @pl.when((s >= 1) & (s <= last))
+        def _():
+            each(s - 1, cross)
+
+        @pl.when(s == last + 1)
+        def _():
+            cross(i)
+
+        @pl.when(s >= 2)
+        def _():
+            sums(s - 2)
 
     ready(i)
 
@@ -231,7 +273,7 @@
 
     here_kv = width // HD
     per = n_intra // KV
-    acc = total_of(0) + bkv[...].astype(jnp.float32)
+    acc = total_of(0) + bkv[...].astype(jnp.float32)[None, :]
     for b in range(here_kv):
         gb = j * here_kv + b
         u = acc[:, b * HD:(b + 1) * HD]
@@ -261,7 +303,7 @@
 
     for c in range(1, chunks):
         base = (c - 1) * width
-        acc = total_of(c) + bq[:, base:base + width].astype(jnp.float32)
+        acc = total_of(c) + bq[base:base + width].astype(jnp.float32)[None, :]
         for h in range(width // HD):
             qh = rot(acc[:, h * HD:(h + 1) * HD]).astype(jnp.bfloat16)
             for b in range(batches):
@@ -277,13 +319,16 @@
                 out[lo:lo + block, base + h * HD:base + (h + 1) * HD] = ctx.astype(jnp.bfloat16)
 
     for gg in range(layers_each):
-        layer = j * layers_each + gg
         for p in range(n_intra):
-            src, dst = spread(gg, p)
-
-            @pl.when(jnp.logical_not((layer == i) & (p == j)))
-            def _():
-                remote(src, dst, hsend.at[gg * n_intra + p], hrecv.at[i], layer, p).wait_send()
+            here, straight, keep, direct, detour = spread(gg, p)
+
+            @pl.when(straight)
+            def _():
+                direct.wait_send()
+
+            @pl.when(jnp.logical_not(here | straight))
+            def _():
+                detour.wait_send()
 
     @pl.loop(0, n_inter)
     def _(t):
@@ -292,6 +337,10 @@
 
         @pl.when(t != i)
         def _():
+            @pl.when(detoured(t))
+            def _():
+                along(t).wait_send()
+
             @pl.loop(0, chunks)
             def _(c):
                 chain(t, c, t, i).wait_send()
@@ -312,9 +361,6 @@
     width = w_keyval.shape[1]
     chunks = 1 + cols // width
     chips = n_intra // CORES
-    half = HD // 2
-    fr = 1000000.0 ** (-2.0 * np.arange(half, dtype=np.float64) / HD)
-    freq = jnp.asarray(np.concatenate([fr, fr])[None, :], jnp.float32)
     vmem = pl.BlockSpec(memory_space=pltpu.VMEM)
     hbm = pl.BlockSpec(memory_space=pl.ANY)
     dma = pltpu.SemaphoreType.DMA
@@ -323,10 +369,11 @@
     result = pl.pallas_call(
         functools.partial(kernel, n_inter, n_intra),
         out_shape=jax.ShapeDtypeStruct((rows, cols), jnp.bfloat16),
-        in_specs=[hbm, hbm, hbm, vmem, vmem, vmem, vmem],
+        in_specs=[hbm, hbm, hbm, vmem, vmem, vmem],
         out_specs=vmem,
         scratch_shapes=[
             pltpu.VMEM((n_inter, rows, depth), jnp.bfloat16),
+            pltpu.VMEM((n_inter, rows // n_intra, depth), jnp.bfloat16),
             pltpu.VMEM((chunks, depth, width), jnp.bfloat16),
             pltpu.VMEM((n_inter + 1, chunks, rows, width), jnp.bfloat16),
             pltpu.VMEM((rows, HD), jnp.float32),
@@ -336,6 +383,8 @@
             pltpu.VMEM((2, rows, HD), jnp.bfloat16),
             dma((chunks,)),
             dma((n_intra * (n_inter // n_intra),)),
+            dma((n_inter,)),
+            dma((n_inter,)),
             dma((n_inter,)),
             dma((n_inter, chips)),
             dma((n_inter, max(chips - 1, 1))),
@@ -348,8 +397,7 @@
         compiler_params=pltpu.CompilerParams(
             collective_id=0, has_side_effects=True, vmem_limit_bytes=52 * 2**20),
         name="project_attend",
-    )(hidden.reshape(rows, feats), w_query, w_keyval, b_query[None, :], b_keyval[None, :],
-      segments.reshape(batches, block), freq)
+    )(hidden.reshape(rows, feats), w_query, w_keyval, b_query, b_keyval, segments)
     return result.reshape(batches, block, cols)
 
 

time: 173 us -> 146 us (0.84)
  Pallas kernels: 167 us -> 142 us
    pallas_call x1, Pallas kernels: 167 us -> 142 us  [local(): pl.pallas_call(functools.partial(kernel, n_inter, n_intra), out_shape=jax...]
    unnamed x6 -> x9, local copies, waits for them, and re-layouts: 3.44 us -> 4.12 us
where the time goes in v2:
time: 146 us
  Pallas kernels  142 us (97%)
  local copies, waits for them, and re-layouts  4.12 us (3%)
    pallas_call x1, Pallas kernels, local(): pl.pallas_call(functools.partial(kernel, n_inter, n_intra), out_shape=jax...  142 us
    unnamed x9, local copies, waits for them, and re-layouts  4.12 us

profile of v2, /device:TPU:9, one launch (start us, length us, event | category | flops | bytes accessed | tf_op | source)
XLA Modules:
  0.0 146.2 jit_solution(4049419539104835554)
XLA Ops:
  0.0 0.0 copy-start
  0.0 1.2 copy-done
  1.2 0.0 copy-start.1
  1.2 0.7 copy-done.1
  1.9 0.0 copy-start.2
  1.9 0.7 copy-done.2
  2.6 0.0 copy-start.3
  2.6 0.7 copy-done.3
  3.2 142.1 %project_attend.1 = bf16[384,1024]{1,0:T(8,128)(2,1)S(1)} custom-call(bf16[384,2048]{1,0:T(8,128)(2,1)} %bitcast.3, bf16[2048,1024]{1,0:T(8,128)(2,1)} %wq.1, bf16[2048,256]{1,0:T(8,128)(2,1)S(1)} %copy-done, bf16[1024]{0:T(1024)(128)(2,1)S(1)} %copy-done.1, bf16[256]{0:T(256)(128)(2,1)S(1)} %copy-done.3, s32[2,1,192]{2,1,0:T(1,128)S(1)} %copy-done.2), custom_call_target="tpu_custom_call" | custom-call | tf_op jit(solution)/shard_map/project_attend/pallas_call | solution.py:369
  145.3 0.9 copy.8
Async XLA Ops:
  0.0 1.2 copy-start
  1.2 0.7 copy-start.1
  1.9 0.7 copy-start.2
  2.6 0.7 copy-start.3

commit v3 on v2

--- a/solution.py
+++ b/solution.py
@@ -71,15 +71,14 @@
         straight = jnp.logical_not(here) & ((layer == i) | (p // CORES == xc))
         return here, straight, keep, direct, detour
 
+    def layer_of(gg):
+        return j * layers_each + gg
+
     for gg in range(layers_each):
         for p in range(n_intra):
             here, straight, keep, direct, detour = spread(gg, p)
 
-            @pl.when(here)
-            def _():
-                keep.start()
-
-            @pl.when(straight)
+            @pl.when(straight & (layer_of(gg) != i))
             def _():
                 direct.start()
 
@@ -116,6 +115,18 @@
     @pl.loop(0, n_inter - 1)
     def _(s):
         each(s, onward)
+
+    for gg in range(layers_each):
+        for p in range(n_intra):
+            here, straight, keep, direct, detour = spread(gg, p)
+
+            @pl.when(here)
+            def _():
+                keep.start()
+
+            @pl.when(straight & (layer_of(gg) == i))
+            def _():
+                direct.start()
 
     lane = lax.broadcasted_iota(jnp.int32, (1, HD), 1)
     fr = jnp.exp(lax.rem(lane, HD // 2).astype(jnp.float32) * FALL)

time: 146 us -> 146 us (level)
  no operation moved by 1% of the time
where the time goes in v3:
time: 146 us
  Pallas kernels  142 us (97%)
  local copies, waits for them, and re-layouts  4.12 us (3%)
    pallas_call x1, Pallas kernels, local(): pl.pallas_call(functools.partial(kernel, n_inter, n_intra), out_shape=jax...  142 us
    unnamed x9, local copies, waits for them, and re-layouts  4.12 us

profile of v3, /device:TPU:9, one launch (start us, length us, event | category | flops | bytes accessed | tf_op | source)
XLA Modules:
  0.0 146.2 jit_solution(10609084636828540181)
XLA Ops:
  0.0 0.0 copy-start
  0.0 1.2 copy-done
  1.2 0.0 copy-start.1
  1.2 0.7 copy-done.1
  1.9 0.0 copy-start.2
  1.9 0.7 copy-done.2
  2.6 0.0 copy-start.3
  2.6 0.7 copy-done.3
  3.2 142.0 %project_attend.1 = bf16[384,1024]{1,0:T(8,128)(2,1)S(1)} custom-call(bf16[384,2048]{1,0:T(8,128)(2,1)} %bitcast.3, bf16[2048,1024]{1,0:T(8,128)(2,1)} %wq.1, bf16[2048,256]{1,0:T(8,128)(2,1)S(1)} %copy-done, bf16[1024]{0:T(1024)(128)(2,1)S(1)} %copy-done.1, bf16[256]{0:T(256)(128)(2,1)S(1)} %copy-done.3, s32[2,1,192]{2,1,0:T(1,128)S(1)} %copy-done.2), custom_call_target="tpu_custom_call" | custom-call | tf_op jit(solution)/shard_map/project_attend/pallas_call | solution.py:380
  145.3 0.9 copy.8
Async XLA Ops:
  0.0 1.2 copy-start
  1.2 0.7 copy-start.1
  1.9 0.7 copy-start.2
  2.6 0.7 copy-start.3
